TPU v7x, 32 devices: a whole 2x2x4 slice. The times are simulated.
32 devices in a mesh: row: 4 (over x, core), col: 8 (over z, y).
Axes of the slice: x: 2, y: 2, z: 4, core: 2. Of those that a mesh axis runs over, the one named last changes fastest.
Arguments:
- tokens: bfloat16 [512, 12288], P('col', 'row'), may hold values from -6 to 6
- up_mant: bfloat16 [12288, 24576], P('row', 'col'), may hold values from -0.0546875 to 0.0546875
- up_exp: int32 [24576], P('col'), may hold values from -1 to 1
- down_mant: bfloat16 [24576, 12288], P('col', 'row'), may hold values from -0.0390625 to 0.0390625
- down_exp: int32 [12288], P('row'), may hold values from -1 to 1
- cotangent: bfloat16 [512, 12288], P('col', 'row'), may hold values from -6 to 6
Outputs:
- output: bfloat16 [512, 12288], P('col', 'row')
- grad_tokens: bfloat16 [512, 12288], P('col', 'row')
- grad_up: bfloat16 [12288, 24576], P('row', 'col')
- grad_down: bfloat16 [24576, 12288], P('col', 'row')
All inputs are finite; a program needn't handle non-finite values.
Results may differ from a plain program's by a relative error of at most 0.018.
Values may be sent and summed in bfloat16 or wider, within the bound.
A program may use at most 192 MiB of HBM per device.

v0:
```python
import jax
import jax.numpy as jnp
from jax import lax
from jax.sharding import PartitionSpec as P


def gelu_grad(pre_act, upstream):
    return jax.vjp(jax.nn.gelu, pre_act)[1](upstream)[0]


def shards(tokens, up_mant, up_exp, down_mant, down_exp, cotangent):
    up_scale = jnp.exp2(up_exp.astype(jnp.float32))
    down_scale = jnp.exp2(down_exp.astype(jnp.float32))
    x_full = lax.all_gather(tokens, "col", axis=0, tiled=True)
    up_term = jnp.dot(x_full, up_mant, preferred_element_type=jnp.float32)
    pre_act = (
        lax.psum_scatter(
            up_term.astype(jnp.bfloat16), "row", scatter_dimension=0, tiled=True
        ).astype(jnp.float32)
        * up_scale[None, :]
    )
    hidden_share = jax.nn.gelu(pre_act).astype(jnp.bfloat16)
    hidden_full = lax.all_gather(hidden_share, "row", axis=0, tiled=True)
    picked = hidden_full
    out_sum = lax.psum_scatter(
        jnp.dot(picked, down_mant, preferred_element_type=jnp.float32).astype(jnp.bfloat16),
        "col",
        scatter_dimension=0,
        tiled=True,
    ).astype(jnp.float32)
    output = (out_sum * down_scale[None, :]).astype(jnp.bfloat16)
    grad_share = (cotangent.astype(jnp.float32) * down_scale[None, :]).astype(jnp.bfloat16)
    grad_out = lax.all_gather(grad_share, "col", axis=0, tiled=True)
    grad_down = lax.dot_general(
        hidden_full, grad_out, (((0,), (0,)), ((), ())), preferred_element_type=jnp.float32
    ).astype(jnp.bfloat16)
    back_term = lax.dot_general(
        grad_out, down_mant, (((1,), (1,)), ((), ())), preferred_element_type=jnp.float32
    )
    grad_hidden = lax.psum_scatter(
        back_term.astype(jnp.bfloat16), "row", scatter_dimension=0, tiled=True
    ).astype(jnp.float32)
    mid_share = (gelu_grad(pre_act, grad_hidden) * up_scale[None, :]).astype(jnp.bfloat16)
    grad_mid = lax.all_gather(mid_share, "row", axis=0, tiled=True)
    grad_up = lax.dot_general(
        x_full, grad_mid, (((0,), (0,)), ((), ())), preferred_element_type=jnp.float32
    ).astype(jnp.bfloat16)
    picked = grad_mid
    grad_tokens = lax.psum_scatter(
        lax.dot_general(
            picked, up_mant, (((1,), (1,)), ((), ())), preferred_element_type=jnp.float32
        ).astype(jnp.bfloat16),
        "col",
        scatter_dimension=0,
        tiled=True,
    )
    return (output, grad_tokens, grad_up, grad_down)


def solution(mesh):
    placed = (
        P("col", "row"),
        P("row", "col"),
        P("col"),
        P("col", "row"),
        P("row"),
        P("col", "row"),
    )
    return jax.shard_map(
        shards,
        mesh=mesh,
        in_specs=placed,
        out_specs=(P("col", "row"), P("col", "row"), P("row", "col"), P("col", "row")),
        check_vma=False,
    )
```

profile of v0, /device:TPU:0, one launch (start us, length us, event | category | flops | bytes accessed | tf_op | source)
XLA Modules:
  0.0 441.5 jit_solution(7246562271617380435)
XLA Ops:
  7.2 0.7 multiply_exponential_fusion
  7.9 1.8 multiply_convert_fusion.1
  9.8 0.7 all-gather.5.cloned.1.call-update
  10.6 63.4 %all-gather.9.cloned.1.call-done = bf16[512,3072]{1,0:T(8,128)(2,1)} async-done(((bf16[64,3072]{1,0:T(8,128)(2,1)}), bf16[512,3072]{1,0:T(8,128)(2,1)}) %all-gather.9.cloned.1.call-update) | async-done | bytes 3145744 | tf_op jit(solution)/shard_map/all_gather | solution.py:33
  73.9 15.9 %convolution_convert_fusion.2 = bf16[512,3072]{1,0:T(8,128)(2,1)} fusion(bf16[512,3072]{1,0:T(8,128)(2,1)} %all-gather.9.cloned.1.call-done, bf16[3072,3072]{1,0:T(8,128)(2,1)} %param.9), kind=kOutput, calls=%fused_computation.3 | convolution fusion | flops 9665249280 | bytes 25165824 | tf_op jit(solution)/shard_map/dot_general | solution.py:37
  89.9 45.4 %all-gather.5.cloned.1.call-done = bf16[512,3072]{1,0:T(8,128)(2,1)} async-done(((bf16[64,3072]{1,0:T(8,128)(2,1)}), bf16[512,3072]{1,0:T(8,128)(2,1)}) %all-gather.5.cloned.1.call-update) | async-done | bytes 3145744 | tf_op jit(solution)/shard_map/all_gather | solution.py:14
  135.2 15.9 %convolution_convert_fusion.4 = bf16[512,3072]{1,0:T(8,128)(2,1)} fusion(bf16[512,3072]{1,0:T(8,128)(2,1)} %all-gather.5.cloned.1.call-done, bf16[3072,3072]{1,0:T(8,128)(2,1)} %param.7), kind=kOutput, calls=%fused_computation.5 | convolution fusion | flops 9665249280 | bytes 25165824 | tf_op jit(solution)/shard_map/dot_general | solution.py:15
  151.2 0.6 copy-done
  151.9 23.1 %reduce-scatter.9.cloned.1.call-done = bf16[128,3072]{1,0:T(8,128)(2,1)} async-done(((bf16[512,3072]{1,0:T(8,128)(2,1)}), bf16[128,3072]{1,0:T(8,128)(2,1)}) %reduce-scatter.9.cloned.1.call-update) | async-done | bytes 786448 | tf_op jit(solution)/shard_map/reduce_scatter | solution.py:40
  175.0 41.1 %reduce-scatter.5.cloned.1.call-done = bf16[128,3072]{1,0:T(8,128)(2,1)} async-done(((bf16[512,3072]{1,0:T(8,128)(2,1)}), bf16[128,3072]{1,0:T(8,128)(2,1)}) %reduce-scatter.5.cloned.1.call-update) | async-done | bytes 786448 | tf_op jit(solution)/shard_map/reduce_scatter | solution.py:17
  216.1 3.9 fusion.3
  220.0 0.5 all-gather.11.cloned.1.call-update
  220.6 28.1 %all-gather.7.cloned.1.call-done = bf16[512,3072]{1,0:T(8,128)(2,1)} async-done(((bf16[128,3072]{1,0:T(8,128)(2,1)}), bf16[512,3072]{1,0:T(8,128)(2,1)}) %all-gather.7.cloned.1.call-update) | async-done | bytes 3145744 | tf_op jit(solution)/shard_map/all_gather | solution.py:23
  248.7 15.9 %convolution_convert_fusion.3 = bf16[512,3072]{1,0:T(8,128)(2,1)} fusion(bf16[512,3072]{1,0:T(8,128)(2,1)} %all-gather.7.cloned.1.call-done, bf16[3072,3072]{1,0:T(8,128)(2,1)} %param.9), kind=kOutput, calls=%fused_computation.4 | convolution fusion | flops 9665249280 | bytes 25165824 | tf_op jit(solution)/shard_map/dot_general | solution.py:26
  264.5 0.2 reduce-scatter.11.cloned.1.call-start
  264.8 14.4 %all-gather.11.cloned.1.call-done = bf16[512,3072]{1,0:T(8,128)(2,1)} async-done(((bf16[128,3072]{1,0:T(8,128)(2,1)}), bf16[512,3072]{1,0:T(8,128)(2,1)}) %all-gather.11.cloned.1.call-update) | async-done | bytes 3145744 | tf_op jit(solution)/shard_map/all_gather | solution.py:44
  279.2 16.0 %convolution_convert_fusion.1 = bf16[512,3072]{1,0:T(8,128)(2,1)} fusion(bf16[512,3072]{1,0:T(8,128)(2,1)} %all-gather.11.cloned.1.call-done, bf16[3072,3072]{1,0:T(8,128)(2,1)} %param.7), kind=kOutput, calls=%fused_computation.2 | convolution fusion | flops 9665249280 | bytes 25165824 | tf_op jit(solution)/shard_map/dot_general | solution.py:50
  295.2 1.9 copy-done.2
  297.1 15.1 %convert_bitcast_fusion = bf16[3072,3072]{0,1:T(8,128)(2,1)} fusion(bf16[512,3072]{1,0:T(8,128)(2,1)} %all-gather.11.cloned.1.call-done, bf16[512,3072]{1,0:T(8,128)(2,1)S(1)} %copy-done.2), kind=kOutput, calls=%fused_computation | convolution fusion | flops 9673113600 | bytes 25165824 | tf_op jit(solution)/shard_map/dot_general | solution.py:45
  312.2 24.8 %copy.10 = bf16[3072,3072]{1,0:T(8,128)(2,1)} copy(bf16[3072,3072]{0,1:T(8,128)(2,1)} %convert_bitcast_fusion) | data formatting | bytes 37748736
  337.1 15.1 %convolution_convert_fusion = bf16[3072,3072]{1,0:T(8,128)(2,1)} fusion(bf16[512,3072]{1,0:T(8,128)(2,1)} %all-gather.7.cloned.1.call-done, bf16[512,3072]{1,0:T(8,128)(2,1)S(1)} %copy-done.1), kind=kOutput, calls=%fused_computation.1 | convolution fusion | flops 9673113600 | bytes 25165824 | tf_op jit(solution)/shard_map/dot_general | solution.py:34
  352.2 5.0 %reduce-scatter.7.cloned.1.call-done = bf16[64,3072]{1,0:T(8,128)(2,1)} async-done(((bf16[512,3072]{1,0:T(8,128)(2,1)}), bf16[64,3072]{1,0:T(8,128)(2,1)}) %reduce-scatter.7.cloned.1.call-update) | async-done | bytes 393232 | tf_op jit(solution)/shard_map/reduce_scatter | solution.py:25
  357.1 1.8 multiply_convert_fusion.2
  358.9 75.7 %reduce-scatter.11.cloned.1.call-done = bf16[64,3072]{1,0:T(8,128)(2,1)} async-done(((bf16[512,3072]{1,0:T(8,128)(2,1)}), bf16[64,3072]{1,0:T(8,128)(2,1)}) %reduce-scatter.11.cloned.1.call-update) | async-done | bytes 393232 | tf_op jit(solution)/shard_map/reduce_scatter | solution.py:49
  (18 shorter events, 0.4 us)
Async XLA Ops:
  7.2 66.8 %all-gather.9.cloned.1.call-start = ((), (), s32[]{:S(2)}) async-start(), calls=%async_computation.8 | async-start | bytes 3538944 | tf_op jit(solution)/shard_map/all_gather | solution.py:33
  9.8 125.5 %all-gather.5.cloned.1.call-start = ((), (), s32[]{:S(2)}) async-start(), calls=%async_computation.4 | async-start | bytes 3538944 | tf_op jit(solution)/shard_map/all_gather | solution.py:14
  10.5 164.4 %reduce-scatter.9.cloned.1.call-start = ((), (), s32[]{:S(2)}) async-start(), calls=%async_computation.9 | async-start | bytes 3932160 | tf_op jit(solution)/shard_map/reduce_scatter | solution.py:40
  89.8 126.3 %reduce-scatter.5.cloned.1.call-start = ((), (), s32[]{:S(2)}) async-start(), calls=%async_computation.5 | async-start | bytes 3932160 | tf_op jit(solution)/shard_map/reduce_scatter | solution.py:17
  151.1 0.7 copy-start
  151.2 97.5 %all-gather.7.cloned.1.call-start = ((), (), s32[]{:S(2)}) async-start(), calls=%async_computation.6 | async-start | bytes 3932160 | tf_op jit(solution)/shard_map/all_gather | solution.py:23
  220.0 59.3 %all-gather.11.cloned.1.call-start = ((), (), s32[]{:S(2)}) async-start(), calls=%async_computation.10 | async-start | bytes 3932160 | tf_op jit(solution)/shard_map/all_gather | solution.py:44
  220.5 136.6 %reduce-scatter.7.cloned.1.call-start = ((), (), s32[]{:S(2)}) async-start(), calls=%async_computation.7 | async-start | bytes 3538944 | tf_op jit(solution)/shard_map/reduce_scatter | solution.py:25
  264.5 170.1 %reduce-scatter.11.cloned.1.call-start = ((), (), s32[]{:S(2)}) async-start(), calls=%async_computation.11 | async-start | bytes 3538944 | tf_op jit(solution)/shard_map/reduce_scatter | solution.py:49
  295.2 1.9 copy-start.2
  312.2 24.8 %copy-start.1 = (bf16[512,3072]{1,0:T(8,128)(2,1)S(1)}, bf16[512,3072]{1,0:T(8,128)(2,1)}, u32[]{:S(2)}) copy-start(bf16[512,3072]{1,0:T(8,128)(2,1)} %all-gather.9.cloned.1.call-done) | copy-start | bytes 9437188
Sparse Core Ops, SparseCore 0:
  10.8 63.1 all-gather.8
  76.1 59.0 all-gather.4
  138.3 36.5 reduce-scatter.8
  178.1 37.9 reduce-scatter.4
  220.1 28.5 all-gather.6
  250.6 28.5 all-gather.10
  282.8 74.2 reduce-scatter.6
  361.3 73.3 reduce-scatter.10
where the time goes:
time: 442 us; the launch traced here: 441 us
  waiting for transfers between devices  297 us (67%)
  matrix products  93.8 us (21%)
  local copies, waits for them, and re-layouts  27.3 us (6%)
  between operations  14.1 us (3%)
  other arithmetic  8.2 us (2%)
    reduce_scatter x1, waiting for transfers between devices, shards(): lax.psum_scatter(lax.dot_general(picked, up_mant, (((1,), (1,)), ((), ())...  75.7 us
    all_gather x1, waiting for transfers between devices, shards(): grad_out = lax.all_gather(grad_share, 'col', axis=0, tiled=True)  63.4 us
    all_gather x1, waiting for transfers between devices, shards(): x_full = lax.all_gather(tokens, 'col', axis=0, tiled=True)  45.4 us
    reduce_scatter x1, waiting for transfers between devices, shards(): lax.psum_scatter(up_term.astype(jnp.bfloat16), 'row', scatter_dimension=0...  41.1 us
    all_gather x1, waiting for transfers between devices, shards(): hidden_full = lax.all_gather(hidden_share, 'row', axis=0, tiled=True)  28.1 us
    unnamed x7, local copies, waits for them, and re-layouts  27.3 us
    reduce_scatter x1, waiting for transfers between devices, shards(): lax.psum_scatter(back_term.astype(jnp.bfloat16), 'row', scatter_dimension...  23.1 us
    dot_general x1, matrix products, shards(): lax.dot_general(picked, up_mant, (((1,), (1,)), ((), ())), preferred_elem...  16 us
  transfers between devices with their start and end apart: 8, of which 8 were waited for; matrix products, arithmetic and copies ran while one was open for 27% of the time, Pallas kernels for 0%

commit v1 on v0

v1 whole, which is shorter than its diff:
```python
import functools
import math

import jax
import jax.numpy as jnp
from jax import lax
from jax.experimental import pallas as pl
from jax.experimental.pallas import tpu as pltpu
from jax.sharding import PartitionSpec as P

MESH = pl.DeviceIdType.MESH
F32 = jnp.float32
BF16 = jnp.bfloat16
ROWS = 16
ROOT = math.sqrt(2.0 / math.pi)
CUBIC = 0.044715


def remote(src, dst, send, recv, where):
    return pltpu.make_async_remote_copy(
        src_ref=src, dst_ref=dst, send_sem=send, recv_sem=recv, device_id=where, device_id_type=MESH
    )


def band(index, size):
    return pl.ds(pl.multiple_of(index * size, size), size)


def tiles(rows, body):
    def step(i, carry):
        body(pl.ds(pl.multiple_of(i * ROWS, ROWS), ROWS), i)
        return carry

    lax.fori_loop(0, rows // ROWS, step, 0)


class Ring:
    def __init__(self, n):
        self.n = n
        col = lax.axis_index("col")
        self.col = col
        half = col // 2
        odd = lax.rem(col, 2)
        self.pos = half + odd * (n - 1 - 2 * half)
        self.right = {"col": self.at(1)}
        self.left = {"col": self.at(-1)}

    def at(self, shift):
        q = lax.rem(self.pos + shift + 2 * self.n, self.n)
        return jnp.where(q < self.n // 2, 2 * q, 2 * (self.n - 1 - q) + 1)


class Rows:
    def __init__(self, count):
        self.groups = count // 2
        me = lax.axis_index("row")
        self.me = me
        self.core = lax.rem(me, 2)
        self.group = me // 2
        self.sibling = {"row": me + 1 - 2 * self.core}

    def of(self, shift, core):
        return lax.rem(self.group + shift + 2 * self.groups, self.groups) * 2 + core


def greet(ring, rows):
    partners = []
    if ring is not None:
        partners += [ring.left, ring.right]
    if rows is not None:
        partners += [rows.sibling]
        partners += [{"row": rows.of(d, rows.core)} for d in range(1, rows.groups)]
    barrier = pltpu.get_barrier_semaphore()
    for partner in partners:
        pl.semaphore_signal(barrier, inc=1, device_id=partner, device_id_type=MESH)
    pl.semaphore_wait(barrier, len(partners))


class RingGather:
    def __init__(self, ring, full, send, recv):
        self.ring, self.full, self.send, self.recv = ring, full, send, recv
        self.m = full.shape[0] // ring.n
        self.w = full.shape[1] // 2
        self.last = ring.n // 2 - 1
        self.sent = []
        self.now = None

    def start(self, step):
        ring = self.ring
        self.now = {}
        for way in range(2):
            origin = ring.at(-step if way == 0 else step)
            for h in range(2):
                if step == self.last and h != way:
                    continue
                part = self.full.at[band(origin, self.m), pl.ds(h * self.w, self.w)]
                copy = remote(
                    part, part, self.send.at[way, h, step], self.recv.at[way, h, step],
                    ring.right if way == 0 else ring.left,
                )
                copy.start()
                self.now[way, h] = copy
                self.sent.append(copy)

    def step(self, step):
        ring = self.ring
        before = self.now
        self.now = {}
        for h in range(2):
            for way in range(2):
                before[way, h].wait_recv()
                if step == self.last and h != way:
                    continue
                origin = ring.at(-step if way == 0 else step)
                part = self.full.at[band(origin, self.m), pl.ds(h * self.w, self.w)]
                copy = remote(
                    part, part, self.send.at[way, h, step], self.recv.at[way, h, step],
                    ring.right if way == 0 else ring.left,
                )
                copy.start()
                self.now[way, h] = copy
                self.sent.append(copy)

    def finish(self):
        for copy in self.now.values():
            copy.wait_recv()
        for copy in self.sent:
            copy.wait_send()


def ring_gather_sems(n):
    return [pltpu.SemaphoreType.DMA((2, 2, n // 2))] * 2


def lanes(width):
    return 2 if (width // 4) % 128 == 0 else 1


class RingScatter:
    def __init__(self, ring, part, slots, send, recv):
        self.ring, self.part, self.slots, self.send, self.recv = ring, part, slots, send, recv
        self.m = part.shape[0] // ring.n
        self.k = lanes(part.shape[1])
        self.w = part.shape[1] // (2 * self.k)
        self.sent = []
        self.now = {}

    def columns(self, way, j):
        return pl.ds((way * self.k + j) * self.w, self.w)

    def start(self, step):
        ring = self.ring
        before, self.now = self.now, {}
        for j in range(self.k):
            for way in range(2):
                dest = ring.at(-1 - step if way == 0 else 1 + step)
                own = self.part.at[band(dest, self.m), self.columns(way, j)]
                src = own
                if step > 0:
                    before[way, j].wait_recv()
                    src = self.slots.at[way, step - 1, j]

                    def add(at, i, src=src, own=own):
                        src[at, :] = (src[at, :].astype(F32) + own[at, :].astype(F32)).astype(BF16)

                    tiles(self.m, add)
                copy = remote(
                    src, self.slots.at[way, step, j], self.send.at[way, j, step],
                    self.recv.at[way, j, step], ring.right if way == 0 else ring.left,
                )
                copy.start()
                self.now[way, j] = copy
                self.sent.append(copy)

    def finish(self, scale, out):
        ring = self.ring
        for j in range(self.k):
            for way in range(2):
                self.now[way, j].wait_recv()
                own = self.part.at[band(ring.col, self.m), self.columns(way, j)]
                got = self.slots.at[way, ring.n - 2, j]
                columns = self.columns(way, j)

                def add(at, i, own=own, got=got, columns=columns):
                    total = got[at, :].astype(F32) + own[at, :].astype(F32)
                    if scale is not None:
                        total = total * scale[0:1, columns]
                    out[at, columns] = total.astype(BF16)

                tiles(self.m, add)
        for copy in self.sent:
            copy.wait_send()


def ring_scatter_scratch(n, tokens, width):
    k = lanes(width)
    return [
        pltpu.VMEM((2, n - 1, k, tokens // n, width // (2 * k)), BF16),
        pltpu.SemaphoreType.DMA((2, k, n - 1)),
        pltpu.SemaphoreType.DMA((2, k, n - 1)),
    ]


class RowScatter:
    def __init__(self, rows, part, sib, out, land, send, recv):
        self.rows, self.part, self.sib, self.out, self.land = rows, part, sib, out, land
        self.send, self.recv = send, recv
        self.m = part.shape[0] // (2 * rows.groups)

    def pairs(self):
        rows = self.rows
        g = rows.groups
        self.first = []
        for d in [*range(1, g), 0]:
            chunk = rows.of(d, 1 - rows.core)
            copy = remote(
                self.part.at[band(chunk, self.m), :], self.sib.at[d], self.send.at[0, d],
                self.recv.at[0, d], rows.sibling,
            )
            copy.start()
            self.first.append((d, copy))

    def chips(self):
        rows = self.rows
        self.second = []
        for d, copy in self.first:
            copy.wait_recv()
            if d == 0:
                continue
            own = self.part.at[band(rows.of(d, rows.core), self.m), :]

            def add(at, i, d=d, own=own):
                self.out[d - 1, at, :] = (
                    own[at, :].astype(F32) + self.sib[d, at, :].astype(F32)
                ).astype(BF16)

            tiles(self.m, add)
            far = remote(
                self.out.at[d - 1], self.land.at[d - 1], self.send.at[1, d], self.recv.at[1, d],
                {"row": rows.of(d, rows.core)},
            )
            far.start()
            self.second.append(far)

    def arrived(self):
        for copy in self.second:
            copy.wait_recv()

    def total(self, at, i):
        m = self.m
        own = pl.ds(pl.multiple_of(self.rows.me * m + i * ROWS, ROWS), ROWS)
        value = self.part[own, :].astype(F32) + self.sib[0, at, :].astype(F32)
        for d in range(1, self.rows.groups):
            value += self.land[d - 1, at, :].astype(F32)
        return value

    def finish(self):
        for _, copy in self.first:
            copy.wait_send()
        for copy in self.second:
            copy.wait_send()


def row_scratch(count, tokens, width):
    g = count // 2
    m = tokens // count
    return [
        pltpu.VMEM((g, m, width), BF16),
        pltpu.VMEM((max(g - 1, 1), m, width), BF16),
        pltpu.VMEM((max(g - 1, 1), m, width), BF16),
    ] + [pltpu.SemaphoreType.DMA((2, g))] * 4


class RowGather:
    def __init__(self, rows, full, send, recv):
        self.rows, self.full, self.send, self.recv = rows, full, send, recv
        self.m = full.shape[0] // (2 * rows.groups)

    def to_sibling(self, d):
        part = self.full.at[band(self.rows.of(-d, self.rows.core), self.m), :]
        copy = remote(part, part, self.send.at[0, d], self.recv.at[0, d], self.rows.sibling)
        copy.start()
        return copy

    def start(self):
        rows = self.rows
        part = self.full.at[band(rows.me, self.m), :]
        self.far = []
        for d in range(1, rows.groups):
            copy = remote(
                part, part, self.send.at[1, d], self.recv.at[1, d], {"row": rows.of(d, rows.core)}
            )
            copy.start()
            self.far.append(copy)
        self.near = [self.to_sibling(0)]

    def finish(self):
        for d, copy in enumerate(self.far, 1):
            copy.wait_recv()
            self.near.append(self.to_sibling(d))
        for copy in self.near:
            copy.wait_recv()
        for copy in self.near + self.far:
            copy.wait_send()


def interleave(gather_step, count, row_scatter, middle, row_gather):
    row_scatter.pairs()
    row_scatter.chips()
    half = (2 * count + 2) // 3
    for s in range(1, 1 + half):
        gather_step(s)
    row_scatter.arrived()
    middle()
    row_gather.start()
    for s in range(1 + half, count + 1):
        gather_step(s)


def tokens_kernel(n, share, full, send, recv):
    ring = Ring(n)
    m = share.shape[0]
    full[band(ring.col, m), :] = share[...]
    greet(ring, None)
    gather = RingGather(ring, full, send, recv)
    gather.start(0)
    for s in range(1, n // 2):
        gather.step(s)
    gather.finish()


def forward_kernel(
    n, count, part, share, up_scale, down_scale, hidden, grad_out, pre,
    send, recv, sib, out, land, rs_send, rs_recv, ag_send, ag_recv,
):
    ring, rows = Ring(n), Rows(count)
    m = share.shape[0]
    grad_out[band(ring.col, m), :] = (share[...].astype(F32) * down_scale[0:1, :]).astype(BF16)
    greet(ring, rows)
    scatter = RowScatter(rows, part, sib, out, land, rs_send, rs_recv)
    row_gather = RowGather(rows, hidden, ag_send, ag_recv)
    gather = RingGather(ring, grad_out, send, recv)
    gather.start(0)
    mr = scatter.m

    def middle():
        def body(at, i):
            x = scatter.total(at, i) * up_scale[0:1, :]
            pre[at, :] = x
            h = 0.5 * x * (1.0 + jnp.tanh(ROOT * (x + CUBIC * (x * x * x))))
            mine = pl.ds(pl.multiple_of(rows.me * mr + i * ROWS, ROWS), ROWS)
            hidden[mine, :] = h.astype(BF16)

        tiles(mr, body)

    interleave(gather.step, n // 2 - 1, scatter, middle, row_gather)
    row_gather.finish()
    gather.finish()
    scatter.finish()


def backward_kernel(
    n, count, part, out_part, pre, up_scale, down_scale, mid, output,
    slots, send, recv, sib, out, land, rs_send, rs_recv, ag_send, ag_recv,
):
    ring, rows = Ring(n), Rows(count)
    greet(ring, rows)
    scatter = RowScatter(rows, part, sib, out, land, rs_send, rs_recv)
    row_gather = RowGather(rows, mid, ag_send, ag_recv)
    sums = RingScatter(ring, out_part, slots, send, recv)
    sums.start(0)
    mr = scatter.m

    def middle():
        def body(at, i):
            up = scatter.total(at, i)
            x = pre[at, :]
            t = jnp.tanh(ROOT * (x + CUBIC * (x * x * x)))
            slope = 0.5 * (1.0 + t) + 0.5 * x * (1.0 - t * t) * (ROOT * (1.0 + 3.0 * CUBIC * (x * x)))
            mine = pl.ds(pl.multiple_of(rows.me * mr + i * ROWS, ROWS), ROWS)
            mid[mine, :] = (slope * up * up_scale[0:1, :]).astype(BF16)

        tiles(mr, body)

    interleave(sums.start, n - 2, scatter, middle, row_gather)
    row_gather.finish()
    sums.finish(down_scale, output)
    scatter.finish()


def sum_kernel(n, part, result, slots, send, recv):
    ring = Ring(n)
    greet(ring, None)
    sums = RingScatter(ring, part, slots, send, recv)
    for s in range(n - 1):
        sums.start(s)
    sums.finish(None, result)


def call(body, outs, scratch, number, *operands):
    spec = pl.BlockSpec(memory_space=pltpu.VMEM)
    return pl.pallas_call(
        body,
        out_shape=outs,
        in_specs=[spec] * len(operands),
        out_specs=jax.tree.map(lambda _: spec, outs),
        scratch_shapes=scratch,
        compiler_params=pltpu.CompilerParams(
            collective_id=number, has_side_effects=True, vmem_limit_bytes=48 * 1024 * 1024
        ),
    )(*operands)


def outer_kernel(step, left, right, out):
    def body(j, carry):
        at = pl.ds(pl.multiple_of(j * step, step), step)
        out[:, at] = lax.dot_general(
            left[...], right[:, at], (((0,), (0,)), ((), ())), preferred_element_type=F32
        ).astype(BF16)
        return carry

    lax.fori_loop(0, right.shape[1] // step, body, 0)


def outer(left, right):
    tokens, a = left.shape
    b = right.shape[1]
    ta, tb = math.gcd(a, 512), math.gcd(b, 1024)
    return pl.pallas_call(
        functools.partial(outer_kernel, tb),
        out_shape=jax.ShapeDtypeStruct((a, b), BF16),
        grid=(a // ta,),
        in_specs=[
            pl.BlockSpec((tokens, ta), lambda i: (0, i)),
            pl.BlockSpec((tokens, b), lambda i: (0, 0)),
        ],
        out_specs=pl.BlockSpec((ta, b), lambda i: (i, 0)),
        compiler_params=pltpu.CompilerParams(vmem_limit_bytes=40 * 1024 * 1024),
        cost_estimate=pl.CostEstimate(
            flops=2 * a * b * tokens, bytes_accessed=2 * (a * b + tokens * (a + b)), transcendentals=0
        ),
    )(left, right)


def shards(n, count, tokens, up_mant, up_exp, down_mant, down_exp, cotangent):
    struct = jax.ShapeDtypeStruct
    m, width = tokens.shape
    units = up_mant.shape[1]
    total = m * n
    up_scale = jnp.exp2(up_exp.astype(F32))[None, :]
    down_scale = jnp.exp2(down_exp.astype(F32))[None, :]
    x_full = call(
        functools.partial(tokens_kernel, n), struct((total, width), BF16), ring_gather_sems(n), 0, tokens
    )
    up_term = jnp.dot(x_full, up_mant, preferred_element_type=F32).astype(BF16)
    hidden, grad_out, pre = call(
        functools.partial(forward_kernel, n, count),
        (struct((total, units), BF16), struct((total, width), BF16), struct((total // count, units), F32)),
        ring_gather_sems(n) + row_scratch(count, total, units),
        1, up_term, cotangent, up_scale, down_scale,
    )
    out_term = jnp.dot(hidden, down_mant, preferred_element_type=F32).astype(BF16)
    back_term = lax.dot_general(
        grad_out, down_mant, (((1,), (1,)), ((), ())), preferred_element_type=F32
    ).astype(BF16)
    mid, output = call(
        functools.partial(backward_kernel, n, count),
        (struct((total, units), BF16), struct((m, width), BF16)),
        ring_scatter_scratch(n, total, width) + row_scratch(count, total, units),
        2, back_term, out_term, pre, up_scale, down_scale,
    )
    tokens_term = lax.dot_general(
        mid, up_mant, (((1,), (1,)), ((), ())), preferred_element_type=F32
    ).astype(BF16)
    grad_tokens = call(
        functools.partial(sum_kernel, n), struct((m, width), BF16),
        ring_scatter_scratch(n, total, width), 3, tokens_term,
    )
    return (output, grad_tokens, outer(x_full, mid), outer(hidden, grad_out))


def solution(mesh):
    placed = (P("col", "row"), P("row", "col"), P("col"), P("col", "row"), P("row"), P("col", "row"))
    return jax.shard_map(
        functools.partial(shards, mesh.shape["col"], mesh.shape["row"]),
        mesh=mesh,
        in_specs=placed,
        out_specs=(P("col", "row"), P("col", "row"), P("row", "col"), P("col", "row")),
        check_vma=False,
    )
```

time: 442 us -> 267 us (0.60)
  waiting for transfers between devices: 297 us -> 0 us
  Pallas kernels: 0 us -> 198 us
  matrix products: 93.8 us -> 61.7 us
  local copies, waits for them, and re-layouts: 27.3 us -> 4.17 us
  between operations: 14.1 us -> 0.74 us
  other arithmetic: 8.2 us -> 1.43 us
    pallas_call x0 -> x6, Pallas kernels: none -> 198 us  [the longest x4 168 us: call(): pl.pallas_call(body, out_shape=outs, in_specs=[spec] * len(operands), out...]
    all_gather x4 -> x0, waiting for transfers between devices: 151 us -> none  [the longest x1 63.4 us: shards(): grad_out = lax.all_gather(grad_share, 'col', axis=0, tiled=True)]
    reduce_scatter x4 -> x0, waiting for transfers between devices: 145 us -> none  [the longest x1 75.7 us: shards(): lax.psum_scatter(lax.dot_general(picked, up_mant, (((1,), (1,)), ((), ())...]
    dot_general x5 -> x3, matrix products: 78 us -> 44.7 us  [the longest x1 14.9 us: shards(): up_term = jnp.dot(x_full, up_mant, preferred_element_type=F32).astype(BF16)]
    unnamed x7 -> x16, local copies, waits for them, and re-layouts: 27.3 us -> 4.17 us
    convert_element_type x3 -> x0, other arithmetic: 7.48 us -> none  [the longest x1 3.85 us: shards(): (gelu_grad(pre_act, grad_hidden) * up_scale[None, :]).astype(jnp.bfloat16)]
  transfers between devices with their start and end apart: 8 -> 0, of which waited for: 8 -> 0; matrix products, arithmetic and copies ran while one was open for 27% -> 0% of each run, Pallas kernels for 0% -> 0%
where the time goes in v1:
time: 267 us; the launch traced here: 266 us
  Pallas kernels  198 us (74%)
  matrix products  61.7 us (23%)
  local copies, waits for them, and re-layouts  4.17 us (2%)
    pallas_call x4, Pallas kernels, call(): pl.pallas_call(body, out_shape=outs, in_specs=[spec] * len(operands), out...  168 us
    pallas_call x2, Pallas kernels, outer(): pl.pallas_call(functools.partial(outer_kernel, tb), out_shape=jax.ShapeDt...  30.5 us
    dot_general x1, matrix products, shards(): lax.dot_general(grad_out, down_mant, (((1,), (1,)), ((), ())), preferred_...  17 us
    dot_general x1, matrix products, shards(): up_term = jnp.dot(x_full, up_mant, preferred_element_type=F32).astype(BF16)  14.9 us
    dot_general x1, matrix products, shards(): jnp.dot(hidden, down_mant, preferred_element_type=F32).astype(BF16)  14.9 us
    dot_general x1, matrix products, shards(): lax.dot_general(mid, up_mant, (((1,), (1,)), ((), ())), preferred_element...  14.8 us

profile of v1, /device:TPU:0, one launch (start us, length us, event | category | flops | bytes accessed | tf_op | source)
XLA Modules:
  0.0 266.3 jit_solution(10971453838433995964)
XLA Ops:
  0.6 0.7 multiply_exponential_fusion.1
  1.3 0.7 multiply_exponential_fusion
  2.1 1.0 copy-done
  3.1 36.2 %shard_map.93.left = bf16[512,3072]{1,0:T(8,128)(2,1)S(1)} custom-call(bf16[64,3072]{1,0:T(8,128)(2,1)S(1)} %copy-done), custom_call_target="tpu_custom_call" | custom-call | tf_op jit(solution)/shard_map/pallas_call | solution.py:402
  39.3 0.0 copy-start.1
  39.3 14.9 %convolution_convert_fusion.3.part = bf16[512,3072]{1,0:T(8,128)(2,1)} fusion(bf16[512,3072]{1,0:T(8,128)(2,1)S(1)} %shard_map.93.left, bf16[3072,3072]{1,0:T(8,128)(2,1)} %param.7), kind=kOutput, calls=%fused_computation.3 | convolution fusion | flops 9665249280 | bytes 25165824 | tf_op jit(solution)/shard_map/dot_general | solution.py:455
  54.3 0.0 copy-done.1
  54.3 47.6 %shard_map.94 = (bf16[512,3072]{1,0:T(8,128)(2,1)S(1)}, bf16[512,3072]{1,0:T(8,128)(2,1)}, f32[128,3072]{1,0:T(8,128)S(1)}) custom-call(bf16[512,3072]{1,0:T(8,128)(2,1)} %convolution_convert_fusion.3.part, bf16[64,3072]{1,0:T(8,128)(2,1)S(1)} %copy-done.1, f32[1,3072]{1,0:T(1,128)S(1)} %bitcast.10, f32[1,3072]{1,0:T(1,128)S(1)} %bitcast.12), custom_call_target="tpu_custom_call" | custom-call | tf_op jit(solution)/shard_map/pallas_call | solution.py:402
  101.9 0.0 copy-start.2
  101.9 17.0 %convolution_convert_fusion.2.part = bf16[512,3072]{1,0:T(8,128)(2,1)} fusion(bf16[512,3072]{1,0:T(8,128)(2,1)} %get-tuple-element.9.right, bf16[3072,3072]{1,0:T(8,128)(2,1)} %param.9), kind=kOutput, calls=%fused_computation.2 | convolution fusion | flops 9665249280 | bytes 25165824 | tf_op jit(solution)/shard_map/dot_general | solution.py:463
  118.9 0.0 copy-done.2
  118.9 14.9 %convolution_convert_fusion.1.out_part = bf16[512,3072]{1,0:T(8,128)(2,1)} fusion(bf16[512,3072]{1,0:T(8,128)(2,1)S(1)} %get-tuple-element.10.left, bf16[3072,3072]{1,0:T(8,128)(2,1)} %param.9), kind=kOutput, calls=%fused_computation.1 | convolution fusion | flops 9665249280 | bytes 25165824 | tf_op jit(solution)/shard_map/dot_general | solution.py:462
  133.8 48.3 %shard_map.95 = (bf16[512,3072]{1,0:T(8,128)(2,1)S(1)}, bf16[64,3072]{1,0:T(8,128)(2,1)S(1)}) custom-call(bf16[512,3072]{1,0:T(8,128)(2,1)} %convolution_convert_fusion.2.part, bf16[512,3072]{1,0:T(8,128)(2,1)} %convolution_convert_fusion.1.out_part, f32[128,3072]{1,0:T(8,128)S(1)} %get-tuple-element.11.pre, f32[1,3072]{1,0:T(1,128)S(1)} %bitcast.11, ...), custom_call_target="tpu_custom_call" | custom-call | tf_op jit(solution)/shard_map/pallas_call | solution.py:402
  182.1 0.0 copy-start.5
  182.1 1.7 copy-done.5
  183.8 14.8 %convolution_convert_fusion.part = bf16[512,3072]{1,0:T(8,128)(2,1)S(1)} fusion(bf16[512,3072]{1,0:T(8,128)(2,1)} %copy-done.5, bf16[3072,3072]{1,0:T(8,128)(2,1)} %param.7), kind=kOutput, calls=%fused_computation | convolution fusion | flops 9665249280 | bytes 25165824 | tf_op jit(solution)/shard_map/dot_general | solution.py:472
  198.6 0.0 copy-start.6
  198.6 35.6 %shard_map.96 = bf16[64,3072]{1,0:T(8,128)(2,1)S(1)} custom-call(bf16[512,3072]{1,0:T(8,128)(2,1)S(1)} %convolution_convert_fusion.part), custom_call_target="tpu_custom_call" | custom-call | tf_op jit(solution)/shard_map/pallas_call | solution.py:402
  234.3 0.0 copy-done.6
  234.3 15.3 %shard_map.97 = bf16[3072,3072]{1,0:T(8,128)(2,1)} custom-call(bf16[512,3072]{1,0:T(8,128)(2,1)S(1)} %shard_map.93.left, bf16[512,3072]{1,0:T(8,128)(2,1)S(1)} %copy-done.6), custom_call_target="tpu_custom_call" | custom-call | flops 9663676416 | bytes 25165824 | tf_op jit(solution)/shard_map/pallas_call | solution.py:429
  249.6 0.0 copy-done.3
  249.6 15.3 %shard_map.98 = bf16[3072,3072]{1,0:T(8,128)(2,1)} custom-call(bf16[512,3072]{1,0:T(8,128)(2,1)S(1)} %copy-done.3, bf16[512,3072]{1,0:T(8,128)(2,1)S(1)} %copy-done.4), custom_call_target="tpu_custom_call" | custom-call | flops 9663676416 | bytes 25165824 | tf_op jit(solution)/shard_map/pallas_call | solution.py:429
  264.8 0.7 copy.12
  265.6 0.7 copy.13
  (4 shorter events, 0.0 us)
Async XLA Ops:
  2.1 1.0 copy-start
  39.3 15.0 %copy-start.1 = (bf16[64,3072]{1,0:T(8,128)(2,1)S(1)}, bf16[64,3072]{1,0:T(8,128)(2,1)}, u32[]{:S(2)}) copy-start(bf16[64,3072]{1,0:T(8,128)(2,1)} %share.3) | copy-start | bytes 1179652
  101.9 17.0 %copy-start.2 = (bf16[512,3072]{1,0:T(8,128)(2,1)}, bf16[512,3072]{1,0:T(8,128)(2,1)S(1)}, u32[]{:S(2)}) copy-start(bf16[512,3072]{1,0:T(8,128)(2,1)S(1)} %get-tuple-element.10.left) | copy-start | bytes 9437188
  182.1 1.7 copy-start.5
  198.6 35.7 %copy-start.6 = (bf16[512,3072]{1,0:T(8,128)(2,1)S(1)}, bf16[512,3072]{1,0:T(8,128)(2,1)}, u32[]{:S(2)}) copy-start(bf16[512,3072]{1,0:T(8,128)(2,1)} %copy-done.5) | copy-start | bytes 9437188
  234.3 15.3 %copy-start.3 = (bf16[512,3072]{1,0:T(8,128)(2,1)S(1)}, bf16[512,3072]{1,0:T(8,128)(2,1)}, u32[]{:S(2)}) copy-start(bf16[512,3072]{1,0:T(8,128)(2,1)} %copy-done.2) | copy-start | bytes 9437188
  234.3 15.3 %copy-start.4 = (bf16[512,3072]{1,0:T(8,128)(2,1)S(1)}, bf16[512,3072]{1,0:T(8,128)(2,1)}, u32[]{:S(2)}) copy-start(bf16[512,3072]{1,0:T(8,128)(2,1)} %get-tuple-element.9.right) | copy-start | bytes 9437188

commit v2 on v1

--- a/solution.py
+++ b/solution.py
@@ -144,33 +144,50 @@
         self.w = part.shape[1] // (2 * self.k)
         self.sent = []
         self.now = {}
+        self.done = {}
 
     def columns(self, way, j):
         return pl.ds((way * self.k + j) * self.w, self.w)
 
-    def start(self, step):
+    def order(self):
+        return [(way, j) for j in range(self.k) for way in range(2)]
+
+    def advance(self, chain):
+        way, j = chain
+        step = self.done.get(chain, 0)
+        if step == self.ring.n - 1:
+            return
+        self.done[chain] = step + 1
         ring = self.ring
-        before, self.now = self.now, {}
-        for j in range(self.k):
-            for way in range(2):
-                dest = ring.at(-1 - step if way == 0 else 1 + step)
-                own = self.part.at[band(dest, self.m), self.columns(way, j)]
-                src = own
-                if step > 0:
-                    before[way, j].wait_recv()
-                    src = self.slots.at[way, step - 1, j]
-
-                    def add(at, i, src=src, own=own):
-                        src[at, :] = (src[at, :].astype(F32) + own[at, :].astype(F32)).astype(BF16)
-
-                    tiles(self.m, add)
-                copy = remote(
-                    src, self.slots.at[way, step, j], self.send.at[way, j, step],
-                    self.recv.at[way, j, step], ring.right if way == 0 else ring.left,
-                )
-                copy.start()
-                self.now[way, j] = copy
-                self.sent.append(copy)
+        dest = ring.at(-1 - step if way == 0 else 1 + step)
+        own = self.part.at[band(dest, self.m), self.columns(way, j)]
+        src = own
+        if step > 0:
+            self.now[chain].wait_recv()
+            src = self.slots.at[way, step - 1, j]
+
+            def add(at, i):
+                src[at, :] = (src[at, :].astype(F32) + own[at, :].astype(F32)).astype(BF16)
+
+            tiles(self.m, add)
+        copy = remote(
+            src, self.slots.at[way, step, j], self.send.at[way, j, step],
+            self.recv.at[way, j, step], ring.right if way == 0 else ring.left,
+        )
+        copy.start()
+        self.now[chain] = copy
+        self.sent.append(copy)
+
+    def with_product(self, product):
+        for i, chain in enumerate(self.order()):
+            product.columns(chain)
+            self.advance(chain)
+            for earlier in self.order()[:i]:
+                self.advance(earlier)
+
+    def round(self):
+        for chain in self.order():
+            self.advance(chain)
 
     def finish(self, scale, out):
         ring = self.ring
@@ -198,6 +215,50 @@
         pltpu.VMEM((2, n - 1, k, tokens // n, width // (2 * k)), BF16),
         pltpu.SemaphoreType.DMA((2, k, n - 1)),
         pltpu.SemaphoreType.DMA((2, k, n - 1)),
+    ]
+
+
+class Product:
+    def __init__(self, sums, left, weights, held, sem):
+        self.sums, self.left, self.weights, self.held, self.sem = sums, left, weights, held, sem
+
+    def fetch(self, chain):
+        way, j = chain
+        at = self.sums.columns(way, j)
+        source = self.weights.at[:, at]
+        return pltpu.make_async_copy(source, self.held.at[way, j], self.sem.at[way, j])
+
+    def start(self):
+        for chain in self.sums.order():
+            self.fetch(chain).start()
+
+    def columns(self, chain):
+        way, j = chain
+        self.fetch(chain).wait()
+        w = self.sums.w
+        size = math.gcd(w, 256)
+        first = (way * self.sums.k + j) * w
+
+        def body(t, carry):
+            at = pl.ds(pl.multiple_of(t * size, size), size)
+            block = self.held[way, j, :, at]
+            value = lax.dot_general(
+                self.left[...], block, (((1,), (0,)), ((), ())),
+                preferred_element_type=F32,
+            )
+            self.sums.part[:, pl.ds(pl.multiple_of(first + t * size, size), size)] = value.astype(BF16)
+            return carry
+
+        lax.fori_loop(0, w // size, body, 0)
+
+
+def product_scratch(tokens, depth, width):
+    k = lanes(width)
+    w = width // (2 * k)
+    return [
+        pltpu.VMEM((2, k, depth, w), BF16),
+        pltpu.SemaphoreType.DMA((2, k)),
+        pltpu.VMEM((tokens, width), BF16),
     ]
 
 
@@ -294,10 +355,12 @@
             self.far.append(copy)
         self.near = [self.to_sibling(0)]
 
-    def finish(self):
+    def forward(self):
         for d, copy in enumerate(self.far, 1):
             copy.wait_recv()
             self.near.append(self.to_sibling(d))
+
+    def finish(self):
         for copy in self.near:
             copy.wait_recv()
         for copy in self.near + self.far:
@@ -354,21 +417,22 @@
         tiles(mr, body)
 
     interleave(gather.step, n // 2 - 1, scatter, middle, row_gather)
+    row_gather.forward()
+    gather.finish()
     row_gather.finish()
-    gather.finish()
     scatter.finish()
 
 
 def backward_kernel(
-    n, count, part, out_part, pre, up_scale, down_scale, mid, output,
-    slots, send, recv, sib, out, land, rs_send, rs_recv, ag_send, ag_recv,
+    n, count, part, hidden, pre, up_scale, down_scale, down_mant, mid, output,
+    held, held_sem, out_part, slots, send, recv, sib, out, land, rs_send, rs_recv, ag_send, ag_recv,
 ):
     ring, rows = Ring(n), Rows(count)
     greet(ring, rows)
     scatter = RowScatter(rows, part, sib, out, land, rs_send, rs_recv)
     row_gather = RowGather(rows, mid, ag_send, ag_recv)
     sums = RingScatter(ring, out_part, slots, send, recv)
-    sums.start(0)
+    product = Product(sums, hidden, down_mant, held, held_sem)
     mr = scatter.m
 
     def middle():
@@ -382,9 +446,19 @@
 
         tiles(mr, body)
 
-    interleave(sums.start, n - 2, scatter, middle, row_gather)
+    scatter.pairs()
+    product.start()
+    scatter.chips()
+    sums.with_product(product)
+    scatter.arrived()
+    middle()
+    row_gather.start()
+    for s in range(n - 2):
+        sums.round()
+        if s == n // 2 - 1:
+            row_gather.forward()
+    sums.finish(down_scale, output)
     row_gather.finish()
-    sums.finish(down_scale, output)
     scatter.finish()
 
 
@@ -393,22 +467,22 @@
     greet(ring, None)
     sums = RingScatter(ring, part, slots, send, recv)
     for s in range(n - 1):
-        sums.start(s)
+        sums.round()
     sums.finish(None, result)
 
 
-def call(body, outs, scratch, number, *operands):
+def call(body, outs, scratch, number, *operands, weights=()):
     spec = pl.BlockSpec(memory_space=pltpu.VMEM)
     return pl.pallas_call(
         body,
         out_shape=outs,
-        in_specs=[spec] * len(operands),
+        in_specs=[spec] * len(operands) + [pl.BlockSpec(memory_space=pl.ANY)] * len(weights),
         out_specs=jax.tree.map(lambda _: spec, outs),
         scratch_shapes=scratch,
         compiler_params=pltpu.CompilerParams(
-            collective_id=number, has_side_effects=True, vmem_limit_bytes=48 * 1024 * 1024
+            collective_id=number, has_side_effects=True, vmem_limit_bytes=52 * 1024 * 1024
         ),
-    )(*operands)
+    )(*operands, *weights)
 
 
 def outer_kernel(step, left, right, out):
@@ -459,15 +533,16 @@
         ring_gather_sems(n) + row_scratch(count, total, units),
         1, up_term, cotangent, up_scale, down_scale,
     )
-    out_term = jnp.dot(hidden, down_mant, preferred_element_type=F32).astype(BF16)
     back_term = lax.dot_general(
         grad_out, down_mant, (((1,), (1,)), ((), ())), preferred_element_type=F32
     ).astype(BF16)
     mid, output = call(
         functools.partial(backward_kernel, n, count),
         (struct((total, units), BF16), struct((m, width), BF16)),
-        ring_scatter_scratch(n, total, width) + row_scratch(count, total, units),
-        2, back_term, out_term, pre, up_scale, down_scale,
+        product_scratch(total, units, width)
+        + ring_scatter_scratch(n, total, width)
+        + row_scratch(count, total, units),
+        2, back_term, hidden, pre, up_scale, down_scale, weights=(down_mant,),
     )
     tokens_term = lax.dot_general(
         mid, up_mant, (((1,), (1,)), ((), ())), preferred_element_type=F32

time: 267 us -> 266 us (level)
  Pallas kernels: 198 us -> 211 us
  matrix products: 61.7 us -> 50.3 us
    dot_general x1 -> x0, matrix products: 14.9 us -> none  [shards(): jnp.dot(hidden, down_mant, preferred_element_type=F32).astype(BF16)]
    pallas_call x4, Pallas kernels: 168 us -> 180 us  [call(): pl.pallas_call(body, out_shape=outs, in_specs=[spec] * len(operands) + [p...]
    dot_general x1, matrix products: 14.8 us -> 18.6 us  [shards(): lax.dot_general(mid, up_mant, (((1,), (1,)), ((), ())), preferred_element...]
where the time goes in v2:
time: 266 us
  Pallas kernels  211 us (79%)
  matrix products  50.3 us (19%)
    pallas_call x4, Pallas kernels, call(): pl.pallas_call(body, out_shape=outs, in_specs=[spec] * len(operands) + [p...  180 us
    pallas_call x2, Pallas kernels, outer(): pl.pallas_call(functools.partial(outer_kernel, tb), out_shape=jax.ShapeDt...  30.5 us
    dot_general x1, matrix products, shards(): lax.dot_general(mid, up_mant, (((1,), (1,)), ((), ())), preferred_element...  18.6 us
    dot_general x1, matrix products, shards(): lax.dot_general(grad_out, down_mant, (((1,), (1,)), ((), ())), preferred_...  15.9 us
    dot_general x1, matrix products, shards(): up_term = jnp.dot(x_full, up_mant, preferred_element_type=F32).astype(BF16)  15.8 us

profile of v2, /device:TPU:0, one launch (start us, length us, event | category | flops | bytes accessed | tf_op | source)
XLA Modules:
  0.0 265.8 jit_solution(459738362645306035)
XLA Ops:
  0.6 0.7 multiply_exponential_fusion.1
  1.3 0.7 multiply_exponential_fusion
  2.1 0.0 copy-start.2
  2.1 1.0 copy-done.2
  3.1 37.9 %shard_map.93.left = bf16[512,3072]{1,0:T(8,128)(2,1)} custom-call(bf16[64,3072]{1,0:T(8,128)(2,1)S(1)} %copy-done.2), custom_call_target="tpu_custom_call" | custom-call | tf_op jit(solution)/shard_map/pallas_call | solution.py:476
  40.9 0.0 copy-start.3
  41.0 15.8 %convolution_convert_fusion.2.part = bf16[512,3072]{1,0:T(8,128)(2,1)} fusion(bf16[512,3072]{1,0:T(8,128)(2,1)} %shard_map.93.left, bf16[3072,3072]{1,0:T(8,128)(2,1)} %param.7), kind=kOutput, calls=%fused_computation.2 | convolution fusion | flops 9665249280 | bytes 25165824 | tf_op jit(solution)/shard_map/dot_general | solution.py:529
  56.8 0.0 copy-done.3
  56.8 48.6 %shard_map.94 = (bf16[512,3072]{1,0:T(8,128)(2,1)}, bf16[512,3072]{1,0:T(8,128)(2,1)}, f32[128,3072]{1,0:T(8,128)S(1)}) custom-call(bf16[512,3072]{1,0:T(8,128)(2,1)} %convolution_convert_fusion.2.part, bf16[64,3072]{1,0:T(8,128)(2,1)S(1)} %copy-done.3, f32[1,3072]{1,0:T(1,128)S(1)} %bitcast.8, f32[1,3072]{1,0:T(1,128)S(1)} %bitcast.10), custom_call_target="tpu_custom_call" | custom-call | tf_op jit(solution)/shard_map/pallas_call | solution.py:476
  105.4 15.9 %convolution_convert_fusion.1.part = bf16[512,3072]{1,0:T(8,128)(2,1)} fusion(bf16[512,3072]{1,0:T(8,128)(2,1)} %get-tuple-element.9.right, bf16[3072,3072]{1,0:T(8,128)(2,1)} %down_mant.1), kind=kOutput, calls=%fused_computation.1 | convolution fusion | flops 9665249280 | bytes 25165824 | tf_op jit(solution)/shard_map/dot_general | solution.py:536
  121.3 58.8 %shard_map.95 = (bf16[512,3072]{1,0:T(8,128)(2,1)}, bf16[64,3072]{1,0:T(8,128)(2,1)S(1)}) custom-call(bf16[512,3072]{1,0:T(8,128)(2,1)} %convolution_convert_fusion.1.part, bf16[512,3072]{1,0:T(8,128)(2,1)} %get-tuple-element.10.hidden.left, f32[128,3072]{1,0:T(8,128)S(1)} %get-tuple-element.11.pre, f32[1,3072]{1,0:T(1,128)S(1)} %bitcast.9, ...), custom_call_target="tpu_custom_call" | custom-call | tf_op jit(solution)/shard_map/pallas_call | solution.py:476
  180.2 0.0 copy-start.5
  180.2 18.6 %convolution_convert_fusion.part = bf16[512,3072]{1,0:T(8,128)(2,1)} fusion(bf16[512,3072]{1,0:T(8,128)(2,1)} %get-tuple-element.13.right, bf16[3072,3072]{1,0:T(8,128)(2,1)} %param.7), kind=kOutput, calls=%fused_computation | convolution fusion | flops 9665249280 | bytes 25165824 | tf_op jit(solution)/shard_map/dot_general | solution.py:547
  198.8 34.9 %shard_map.96 = bf16[64,3072]{1,0:T(8,128)(2,1)S(1)} custom-call(bf16[512,3072]{1,0:T(8,128)(2,1)} %convolution_convert_fusion.part), custom_call_target="tpu_custom_call" | custom-call | tf_op jit(solution)/shard_map/pallas_call | solution.py:476
  233.7 0.0 copy-done.5
  233.7 0.0 copy-done
  233.7 0.0 copy-start.1
  233.7 0.0 copy-start.4
  233.7 15.3 %shard_map.97 = bf16[3072,3072]{1,0:T(8,128)(2,1)} custom-call(bf16[512,3072]{1,0:T(8,128)(2,1)S(1)} %copy-done, bf16[512,3072]{1,0:T(8,128)(2,1)S(1)} %copy-done.5), custom_call_target="tpu_custom_call" | custom-call | flops 9663676416 | bytes 25165824 | tf_op jit(solution)/shard_map/pallas_call | solution.py:503
  249.0 0.0 copy-done.1
  249.0 0.0 copy-done.4
  249.0 15.3 %shard_map.98 = bf16[3072,3072]{1,0:T(8,128)(2,1)} custom-call(bf16[512,3072]{1,0:T(8,128)(2,1)S(1)} %copy-done.1, bf16[512,3072]{1,0:T(8,128)(2,1)S(1)} %copy-done.4), custom_call_target="tpu_custom_call" | custom-call | flops 9663676416 | bytes 25165824 | tf_op jit(solution)/shard_map/pallas_call | solution.py:503
  264.3 0.7 copy.12
  265.0 0.7 copy.13
  (1 shorter events, 0.0 us)
Async XLA Ops:
  2.1 1.0 copy-start.2
  40.9 15.9 %copy-start.3 = (bf16[64,3072]{1,0:T(8,128)(2,1)S(1)}, bf16[64,3072]{1,0:T(8,128)(2,1)}, u32[]{:S(2)}) copy-start(bf16[64,3072]{1,0:T(8,128)(2,1)} %share.3) | copy-start | bytes 1179652
  180.2 53.5 %copy-start.5 = (bf16[512,3072]{1,0:T(8,128)(2,1)S(1)}, bf16[512,3072]{1,0:T(8,128)(2,1)}, u32[]{:S(2)}) copy-start(bf16[512,3072]{1,0:T(8,128)(2,1)} %get-tuple-element.13.right) | copy-start | bytes 9437188
  198.8 35.0 %copy-start = (bf16[512,3072]{1,0:T(8,128)(2,1)S(1)}, bf16[512,3072]{1,0:T(8,128)(2,1)}, u32[]{:S(2)}) copy-start(bf16[512,3072]{1,0:T(8,128)(2,1)} %shard_map.93.left) | copy-start | bytes 9437188
  233.7 15.3 %copy-start.1 = (bf16[512,3072]{1,0:T(8,128)(2,1)S(1)}, bf16[512,3072]{1,0:T(8,128)(2,1)}, u32[]{:S(2)}) copy-start(bf16[512,3072]{1,0:T(8,128)(2,1)} %get-tuple-element.10.hidden.left) | copy-start | bytes 9437188
  233.7 15.3 %copy-start.4 = (bf16[512,3072]{1,0:T(8,128)(2,1)S(1)}, bf16[512,3072]{1,0:T(8,128)(2,1)}, u32[]{:S(2)}) copy-start(bf16[512,3072]{1,0:T(8,128)(2,1)} %get-tuple-element.9.right) | copy-start | bytes 9437188
